TPU v7x, 32 devices: a whole 2x2x4 slice. The times are simulated.
32 devices in a mesh: ka: 8 (over z, y), ga: 4 (over x, core).
Axes of the slice: x: 2, y: 2, z: 4, core: 2. Of those that a mesh axis runs over, the one named last changes fastest.
Arguments:
- cond: bfloat16 [8, 8, 4096], P('ka', None, 'ga'), may hold values from -6 to 6
- vale: bfloat16 [8, 8, 4096], P('ka', None, 'ga'), may hold values from -6 to 6
- screen: bfloat16 [8, 4096, 4096], P('ka', 'ga'), may hold values from -0.0014648438 to 0.0014648438
- qtable: int32 [8, 8], replicated, may hold values from 0 to 7, as said below
- gmap: int32 [8, 4096], P('ka', 'ga'), may hold values from 0 to 4095, as said below
Outputs:
- kernel: float32 [8, 3, 4096], P('ka', None, 'ga')
Inputs may be any that keep to these rules, and one draw needn't show every extreme that they name: qtable[k,k2] depends only on (k - k2) mod 8, and each row names every k-difference once. `gmap`: each aligned block of 1024 entries of a row is an ordering of that block's own grid indices.
All inputs are finite; a program needn't handle non-finite values.
Results may differ from a plain program's by a relative error of at most 0.0041.
Values may be sent and summed in bfloat16 or wider, within the bound.
A program may use at most 128 MiB of HBM per device.

v0:
```python
import jax
import jax.numpy as jnp
from jax import lax
from jax.sharding import PartitionSpec as P

NSHIFT = 2


def passed_along(array, axis, by):
    peers = lax.axis_size(axis)
    return lax.ppermute(array, axis, [(i, (i + by) % peers) for i in range(peers)])


def broadcast(value, axis, source):
    kept = jnp.where(lax.axis_index(axis) == source, value, 0).astype(value.dtype)
    return lax.psum(kept, axis)


def pair_density(own, far):
    product = own.astype(jnp.float32)[:, None, :] * far.astype(jnp.float32)[None, :, :]
    return product.astype(jnp.bfloat16).reshape(-1, own.shape[-1])


def per_device(cond, vale, screen, qtable, gmap):
    local_k = cond.shape[0]
    g_width = cond.shape[2]
    cycle_len = lax.axis_size("ka")
    all_k = local_k * cycle_len
    start = lax.axis_index("ga") * g_width
    local_map = gmap - start
    cond_mapped = jnp.take_along_axis(cond, local_map[:, None, :], axis=2)
    vale_mapped = jnp.take_along_axis(vale, local_map[:, None, :], axis=2)
    blocks = {}
    vale_full = lax.all_gather(vale, "ga", axis=2, tiled=True)
    slabs = [(cond_mapped, vale_mapped)]
    for offset in range(NSHIFT):
        previous = slabs[-1]
        slabs.append(passed_along((previous[0], previous[1]), "ka", 1))
    tiles = [(entry[0], lax.all_gather(entry[1], "ga", axis=2, tiled=True)) for entry in slabs]
    for shift_d in range(1 - local_k, (NSHIFT + 1) * local_k):
        pairs = [
            (offset, left, right)
            for offset in range(NSHIFT + 1)
            for left in range(local_k)
            for right in range(local_k)
            if offset * local_k + left - right == shift_d
        ]
        qindex = qtable[shift_d % all_k, 0]
        owner = qindex // local_k
        holder = qindex % local_k
        slab = broadcast(lax.dynamic_index_in_dim(screen, holder, 0, keepdims=False), "ka", owner)
        stacked = jnp.concatenate(
            [
                pair_density(vale_full[left], tiles[offset][1][right])
                for offset, left, right in pairs
            ],
            axis=0,
        )
        image = lax.dot_general(
            slab, stacked, (((1,), (1,)), ((), ())), preferred_element_type=jnp.float32
        )
        for number, (offset, left, right) in enumerate(pairs):
            dens_c = pair_density(cond[left], tiles[offset][0][right])
            tile = jnp.dot(dens_c.astype(jnp.float32), image, precision=lax.Precision.HIGHEST)
            blocks[left, offset * local_k + right] = tile.reshape(-1)
    terms = jnp.stack([jnp.stack([blocks[0, column] for column in range((NSHIFT + 1) * local_k)])])
    return lax.psum_scatter(terms, "ga", scatter_dimension=2, tiled=True)


def solution(mesh):
    in_specs = (P("ka", None, "ga"), P("ka", None, "ga"), P("ka", "ga", None), P(), P("ka", "ga"))
    out_specs = P("ka", None, "ga")
    return jax.shard_map(
        per_device, mesh=mesh, in_specs=in_specs, out_specs=out_specs, check_vma=False
    )
```

profile of v0, /device:TPU:0, one launch (start us, length us, event | category | flops | bytes accessed | tf_op | source)
XLA Modules:
  0.0 870.8 jit_solution(16399893429373409430)
XLA Ops:
  6.5 1.4 fusion.30
  9.8 11.0 %select_bitcast_fusion.2 = (bf16[1024,4096]{1,0:T(8,128)(2,1)}, bf16[1024,4096]{1,0:T(8,128)(2,1)}, bf16[1024,4096]{1,0:T(8,128)(2,1)}) fusion(bf16[1,1024,4096]{2,1,0:T(8,128)(2,1)} %param.9, pred[]{:T(512)S(6)} %eq.13, pred[]{:T(512)S(6)} %eq.15, pred[]{:T(512)S(6)} %eq.14), kind=kLoop, calls=%fused_computation.5 | loop fusion | flops 12582912 | bytes 33554436 | tf_op jit(solution)/shard_map/jit(_where)/select_n | solution.py:15
  20.9 0.6 copy-done.3
  21.9 3.2 gather_fusion
  25.2 3.2 gather_fusion.1
  28.4 0.9 bitcast_convert_fusion.5
  29.3 3.0 collective-permute-start.1
  32.2 1.5 collective-permute-start
  33.8 5.2 all_gather.12
  39.0 10.1 %all_gather.13 = bf16[1,8,4096]{1,2,0:T(8,128)(2,1)S(1)} all-gather(bf16[1,8,1024]{1,2,0:T(8,128)(2,1)S(1)} %get-tuple-element.19), channel_id=1, replica_groups=mesh['ka'=8,'ga'=4] {'ga'}, dimensions={2}, use_global_device_ids=true | all-gather | bytes 81920 | tf_op jit(solution)/shard_map/all_gather | solution.py:39
  49.1 0.7 bitcast_convert_fusion.6
  49.9 1.2 copy.17
  51.3 10.1 %all_gather.14 = bf16[1,8,4096]{1,2,0:T(8,128)(2,1)S(1)} all-gather(bf16[1,8,1024]{1,2,0:T(8,128)(2,1)S(1)} %collective-permute-done.1), channel_id=1, replica_groups=mesh['ka'=8,'ga'=4] {'ga'}, dimensions={2}, use_global_device_ids=true | all-gather | bytes 81920 | tf_op jit(solution)/shard_map/all_gather | solution.py:39
  61.6 1.6 collective-permute-start.3
  63.2 1.2 copy.19
  64.6 1.5 collective-permute-start.2
  66.1 13.0 %collective-permute-done.3 = bf16[1,8,1024]{1,2,0:T(8,128)(2,1)S(1)} collective-permute-done((bf16[1,8,1024]{1,2,0:T(8,128)(2,1)S(1)}, bf16[1,8,1024]{1,2,0:T(8,128)(2,1)S(1)}, u32[]{:S(2)}, u32[]{:S(2)}) %collective-permute-start.3) | collective-permute-done | bytes 16416 | tf_op jit(solution)/shard_map/ppermute | solution.py:11
  79.1 10.2 %all_gather.15 = bf16[1,8,4096]{1,2,0:T(8,128)(2,1)S(1)} all-gather(bf16[1,8,1024]{1,2,0:T(8,128)(2,1)S(1)} %collective-permute-done.3), channel_id=1, replica_groups=mesh['ka'=8,'ga'=4] {'ga'}, dimensions={2}, use_global_device_ids=true | all-gather | bytes 81920 | tf_op jit(solution)/shard_map/all_gather | solution.py:39
  89.5 0.6 copy.21
  90.0 0.2 collective-permute-done.2
  90.4 705.1 %all-reduce.3.cloned.1.call-done = (bf16[1024,4096]{1,0:T(8,128)(2,1)}, bf16[1024,4096]{1,0:T(8,128)(2,1)}, bf16[1024,4096]{1,0:T(8,128)(2,1)}) async-done(((bf16[1024,4096]{1,0:T(8,128)(2,1)}, bf16[1024,4096]{1,0:T(8,128)(2,1)}, bf16[1024,4096]{1,0:T(8,128)(2,1)}), (bf16[1024,4096]{1,0:T(8,128)(2,1)}, bf16[1024,4096]{1,0:T(8,128)(2,1)}, bf16[1024,4096]{1,0:T(8,128)(2,1)})) %all-reduce.3.cloned.1.call-update) | async-done | bytes 25165840 | tf_op jit(solution)/shard_map/psum | solution.py:16
  795.6 5.8 fusion.4
  801.4 0.3 fusion.19
  801.8 5.7 fusion.7
  807.5 0.3 fusion.22
  807.9 5.7 fusion.1
  813.6 0.3 fusion.16
  814.1 5.9 copy.22
  820.0 9.8 %bitcast_reduce_fusion = f32[4096,3]{1,0:T(8,128)} fusion(f32[1,3,4096]{0,1,2:T(4,128)} %copy.22), kind=kLoop, calls=%fused_computation.2 | loop fusion | bytes 98304
  829.9 30.6 %reduce-scatter.4.cloned.1.call-done = f32[1024,3]{1,0:T(8,128)} async-done(((f32[4096,3]{1,0:T(8,128)}), f32[1024,3]{1,0:T(8,128)}) %reduce-scatter.4.cloned.1.call-update) | async-done | bytes 12304
  860.5 2.2 reshape_bitcast_fusion
  862.6 1.3 copy.23
  (33 shorter events, 1.8 us)
Async XLA Ops:
  6.5 789.0 %all-reduce.3.cloned.1.call-start = ((), (), s32[]{:S(2)}) async-start(), calls=%async_computation.2 | async-start | bytes 50331648 | tf_op jit(solution)/shard_map/psum | solution.py:16
  20.8 0.7 copy-start.3
  20.8 0.9 copy-start.2
  20.8 1.1 copy-start.4
  20.8 839.6 %reduce-scatter.4.cloned.1.call-start = ((), (), s32[]{:S(2)}) async-start(), calls=%async_computation.1 | async-start | bytes 2621440
  29.3 22.0 %collective-permute-start.1 = (bf16[1,8,1024]{1,2,0:T(8,128)(2,1)S(1)}, bf16[1,8,1024]{1,2,0:T(8,128)(2,1)S(1)}, u32[]{:S(2)}, u32[]{:S(2)}) collective-permute-start(bf16[1,8,1024]{1,2,0:T(8,128)(2,1)S(1)} %get-tuple-element.19), channel_id=1, source_target_pairs={{0,4},{4,8},{8,12},{12,16},{16,20},{20,24},{24,28},{28,0},{1,5},{5... | collective-permute-start | bytes 49160 | tf_op jit(solution)/shard_map/ppermute | solution.py:11
  32.2 30.9 %collective-permute-start = (bf16[1,8,1024]{1,2,0:T(8,128)(2,1)}, bf16[1,8,1024]{1,2,0:T(8,128)(2,1)S(1)}, u32[]{:S(2)}, u32[]{:S(2)}) collective-permute-start(bf16[1,8,1024]{1,2,0:T(8,128)(2,1)} %get-tuple-element.10), channel_id=1, source_target_pairs={{0,4},{4,8},{8,12},{12,16},{16,20},{20,24},{24,28},{28,0},{1,5},{5... | collective-permute-start | bytes 49160 | tf_op jit(solution)/shard_map/ppermute | solution.py:11
  61.6 17.5 %collective-permute-start.3 = (bf16[1,8,1024]{1,2,0:T(8,128)(2,1)S(1)}, bf16[1,8,1024]{1,2,0:T(8,128)(2,1)S(1)}, u32[]{:S(2)}, u32[]{:S(2)}) collective-permute-start(bf16[1,8,1024]{1,2,0:T(8,128)(2,1)S(1)} %collective-permute-done.1), channel_id=1, source_target_pairs={{0,4},{4,8},{8,12},{12,16},{16,20},{20,24},{24,28},{28,0},{1,5},{5... | collective-permute-start | bytes 49160 | tf_op jit(solution)/shard_map/ppermute | solution.py:11
  64.6 25.6 %collective-permute-start.2 = (bf16[1,8,1024]{1,2,0:T(8,128)(2,1)S(1)}, bf16[1,8,1024]{1,2,0:T(8,128)(2,1)S(1)}, u32[]{:S(2)}, u32[]{:S(2)}) collective-permute-start(bf16[1,8,1024]{1,2,0:T(8,128)(2,1)S(1)} %collective-permute-done), channel_id=1, source_target_pairs={{0,4},{4,8},{8,12},{12,16},{16,20},{20,24},{24,28},{28,0},{1,5},{5... | collective-permute-start | bytes 49160 | tf_op jit(solution)/shard_map/ppermute | solution.py:11
  89.3 712.5 %copy-start.1 = (f32[8,4096]{1,0:T(8,128)S(1)}, f32[8,4096]{1,0:T(8,128)}, u32[]{:S(2)}) copy-start(f32[8,4096]{1,0:T(8,128)} %bitcast_convert_fusion.6) | copy-start | bytes 393220
  795.6 12.4 %copy-start = (f32[8,4096]{1,0:T(8,128)S(1)}, f32[8,4096]{1,0:T(8,128)}, u32[]{:S(2)}) copy-start(f32[8,4096]{1,0:T(8,128)} %copy.17) | copy-start | bytes 393220
Sparse Core Ops, SparseCore 0:
  21.0 774.5 all-reduce.2
  830.0 30.3 reduce-scatter.3
where the time goes:
time: 871 us
  waiting for transfers between devices  749 us (86%)
  blocking collectives  35.7 us (4%)
  local copies, waits for them, and re-layouts  31.7 us (4%)
  matrix products  18.1 us (2%)
  between operations  15.5 us (2%)
  other arithmetic  13.1 us (2%)
    psum x1, waiting for transfers between devices, broadcast(): return lax.psum(kept, axis)  705 us
    unnamed x3, waiting for transfers between devices  30.6 us
    all_gather x3, blocking collectives, per_device(): lax.all_gather(entry[1], 'ga', axis=2, tiled=True)  30.4 us
    unnamed x16, local copies, waits for them, and re-layouts  20.2 us
  transfers between devices with their start and end apart: 6, of which 4 were waited for; matrix products, arithmetic and copies ran while one was open for 1% of the time, Pallas kernels for 0%

commit v1 on v0

v1 whole, which is shorter than its diff:
```python
import functools

import jax
import jax.numpy as jnp
from jax import lax
from jax.experimental import pallas as pl
from jax.experimental.pallas import tpu as pltpu
from jax.sharding import PartitionSpec as P

NSHIFT = 2
MESH = pl.DeviceIdType.MESH
F32 = jnp.float32
BF16 = jnp.bfloat16


def flipped(index, bit):
    width = 1 << bit
    return index + width * (1 - 2 * ((index // width) % 2))


def moved(index, offset, bits):
    for bit in range(bits):
        if (offset >> bit) & 1:
            index = flipped(index, bit)
    return index


def ring_place(ka, peers):
    y, z = ka % 2, ka // 2
    return z * (1 - y) + (peers - 1 - z) * y


def ring_member(place, peers):
    place = (place + 2 * peers) % peers
    late = place // (peers // 2)
    return (1 - late) * 2 * place + late * (2 * (peers - 1 - place) + 1)


def densities(own, far):
    product = own.astype(F32)[:, None, :] * far.astype(F32)[None, :, :]
    return product.reshape(-1, own.shape[-1]).astype(BF16)


def kernel(
    n_k, n_g, cond, vale, screen, qtable, gmap, out,
    s_held, c_all, pc, tiles, sent, got,
    s_sem, c_send, c_recv, v_send, v_recv, g_send, g_recv, t_send, t_recv, *v_from,
):
    bits = n_g.bit_length() - 1
    total = n_k * n_g
    width = cond.shape[2]
    n_c = cond.shape[1]
    rows = n_c * n_c
    me_k, me_g = lax.axis_index("ka"), lax.axis_index("ga")
    me = me_k * n_g + me_g

    barrier = pltpu.get_barrier_semaphore()

    def greet(step, carry):
        peer = (me + step) % total
        pl.semaphore_signal(
            barrier, inc=1, device_id=(peer // n_g, peer % n_g), device_id_type=MESH
        )
        return carry

    lax.fori_loop(1, total, greet, 0)

    loads = []
    for offset in range(n_g):
        block = moved(me_g, offset, bits)
        load = pltpu.make_async_copy(
            screen.at[0, :, pl.ds(pl.multiple_of(block * width, width), width)],
            s_held.at[block],
            s_sem.at[offset],
        )
        load.start()
        loads.append(load)

    local_map = gmap[...] - me_g * width
    both = jnp.concatenate([cond[0], vale[0]], axis=0)
    part = min(256, width)
    mapped = jnp.zeros((2 * n_c, width), F32)
    for first in range(0, width, part):
        points = lax.broadcasted_iota(jnp.int32, (part, width), 0) + first
        pick = jnp.where(points == local_map, 1.0, 0.0).astype(BF16)
        mapped += jnp.dot(both[:, first : first + part], pick, preferred_element_type=F32)
    mapped = mapped.astype(BF16)
    c_all[me_k] = jnp.concatenate([cond[0], mapped[:n_c]], axis=0)
    v_from[0][me_k] = jnp.concatenate([vale[0], mapped[n_c:]], axis=0)

    pl.semaphore_wait(barrier, total - 1)

    place = ring_place(me_k, n_k)
    right, left = ring_member(place + 1, n_k), ring_member(place - 1, n_k)
    n_right, n_left = n_k // 2, n_k - 1 - n_k // 2

    def c_copy(chunk, slot, target):
        return pltpu.make_async_remote_copy(
            src_ref=c_all.at[chunk], dst_ref=c_all.at[chunk],
            send_sem=c_send.at[slot], recv_sem=c_recv.at[chunk],
            device_id=(target, me_g), device_id_type=MESH,
        )

    def v_copy(chunk, slot, target):
        return pltpu.make_async_remote_copy(
            src_ref=v_from[0].at[chunk], dst_ref=v_from[0].at[chunk],
            send_sem=v_send.at[slot], recv_sem=v_recv.at[chunk],
            device_id=(target, me_g), device_id_type=MESH,
        )

    def across(chunk):
        for bit in reversed(range(bits)):
            pltpu.make_async_remote_copy(
                src_ref=v_from[0].at[chunk], dst_ref=v_from[1 << bit].at[chunk],
                send_sem=g_send.at[1 << bit], recv_sem=g_recv.at[1 << bit],
                device_id=(me_k, flipped(me_g, bit)), device_id_type=MESH,
            ).start()

    def whole_block(offset, bit):
        return pltpu.make_async_remote_copy(
            src_ref=v_from[offset], dst_ref=v_from[offset | (1 << bit)],
            send_sem=g_send.at[offset | (1 << bit)], recv_sem=g_recv.at[offset | (1 << bit)],
            device_id=(me_k, flipped(me_g, bit)), device_id_type=MESH,
        )

    c_copy(me_k, 0, right).start()
    c_copy(me_k, n_right, left).start()
    v_copy(me_k, 0, right).start()
    v_copy(me_k, n_right, left).start()
    across(me_k)
    for step in range(1, n_right + 1):
        from_left = ring_member(place - step, n_k)
        from_right = ring_member(place + step, n_k)
        c_copy(from_left, 0, right).wait_recv()
        if step < n_right:
            c_copy(from_left, step, right).start()
        if step <= n_left:
            c_copy(from_right, 0, left).wait_recv()
            if step < n_left:
                c_copy(from_right, n_right + step, left).start()
        v_copy(from_left, 0, right).wait_recv()
        if step < n_right:
            v_copy(from_left, step, right).start()
        across(from_left)
        if step <= n_left:
            v_copy(from_right, 0, left).wait_recv()
            if step < n_left:
                v_copy(from_right, n_right + step, left).start()
            across(from_right)

    shift = jnp.int32(0)
    for row in range(n_k):
        shift = jnp.where(qtable[row, 0] == me_k, row, shift)

    def build(k, carry):
        partner = lax.rem(k - shift + n_k, n_k)
        dens = densities(c_all[k][:n_c], c_all[partner][n_c:])
        pc[pl.ds(pl.multiple_of(k * rows, rows), rows), :] = dens
        return carry

    lax.fori_loop(0, n_k, build, 0)
    tiles[...] = jnp.zeros_like(tiles)

    sub = min(512, width)
    unit = 8
    group = 4
    for offset in range(n_g):
        block = moved(me_g, offset, bits)
        loads[offset].wait()
        if offset:
            low = (offset & -offset).bit_length() - 1
            whole_block(offset & (offset - 1), low).wait_recv()
            for bit in reversed(range(low)):
                whole_block(offset, bit).start()

        def step(number, carry, block=block, held=v_from[offset]):
            which, column = number // (width // sub), number % (width // sub)
            columns = pl.ds(pl.multiple_of(column * sub, sub), sub)
            left_rows = pl.ds(pl.multiple_of(which * (unit * rows), unit * rows), unit * rows)
            weighted = jnp.dot(
                pc[left_rows, :], s_held[block, :, columns], preferred_element_type=F32
            ).astype(BF16)
            for part in range(unit // group):
                dens = []
                for k in range(group):
                    k = which * unit + part * group + k
                    partner = lax.rem(k - shift + n_k, n_k)
                    own = held[k, :, columns][:n_c]
                    far = held[partner, :, columns][n_c:]
                    dens.append(densities(own, far))
                tiles[which * (unit // group) + part] += lax.dot_general(
                    weighted[part * group * rows : (part + 1) * group * rows],
                    jnp.concatenate(dens, axis=0),
                    (((1,), (1,)), ((), ())),
                    preferred_element_type=F32,
                )
            return carry

        lax.fori_loop(0, (n_k // unit) * (width // sub), step, 0)

    share = rows // n_g
    half = share // 2

    def lay_out(which, carry):
        for k in range(group):
            for to in range(n_g):
                first = k * rows + to * share
                lanes = slice(k * rows, (k + 1) * rows)
                sent[(which * group + k) * n_g + to] = jnp.concatenate(
                    [
                        tiles[which, first : first + half, lanes],
                        tiles[which, first + half : first + share, lanes],
                    ],
                    axis=1,
                )
        return carry

    lax.fori_loop(0, n_k // group, lay_out, 0)

    def hand_out(step, carry):
        peer = (me + step) % total
        pltpu.make_async_remote_copy(
            src_ref=sent.at[peer], dst_ref=got.at[me],
            send_sem=t_send, recv_sem=t_recv,
            device_id=(peer // n_g, peer % n_g), device_id_type=MESH,
        ).start()
        return carry

    lax.fori_loop(1, total, hand_out, 0)
    got[me] = sent[me]

    for slot in range(n_k - 1):
        c_copy(me_k, slot, right).wait_send()
        v_copy(me_k, slot, right).wait_send()
    for offset in range(1, n_g):
        low = (offset & -offset).bit_length() - 1
        whole_block(offset & (offset - 1), low).wait_send()

    handed = pltpu.make_async_remote_copy(
        src_ref=sent.at[pl.ds(0, total - 1)], dst_ref=got.at[pl.ds(0, total - 1)],
        send_sem=t_send, recv_sem=t_recv,
        device_id=(me_k, flipped(me_g, 0)), device_id_type=MESH,
    )
    handed.wait_recv()
    for number in range(NSHIFT + 1):
        holder = qtable[number, 0]
        value = got[holder * n_g]
        for source in range(1, n_g):
            value += got[holder * n_g + source]
        out[number, :half, :] = value[:, :rows]
        out[number, half:, :] = value[:, rows:]
    handed.wait_send()


def per_device(cond, vale, screen, qtable, gmap):
    n_k, n_g = lax.axis_size("ka"), lax.axis_size("ga")
    n_c, width = cond.shape[1], cond.shape[2]
    rows = n_c * n_c
    share = rows // n_g
    total = n_k * n_g
    vmem = pl.BlockSpec(memory_space=pltpu.VMEM)
    dma = pltpu.SemaphoreType.DMA
    result = pl.pallas_call(
        functools.partial(kernel, n_k, n_g),
        out_shape=jax.ShapeDtypeStruct((NSHIFT + 1, share, rows), F32),
        in_specs=[
            vmem, vmem, pl.BlockSpec(memory_space=pl.ANY),
            pl.BlockSpec(memory_space=pltpu.SMEM), vmem,
        ],
        out_specs=vmem,
        scratch_shapes=[
            pltpu.VMEM((n_g, width, width), BF16),
            pltpu.VMEM((n_k, 2 * n_c, width), BF16),
            pltpu.VMEM((n_k * rows, width), BF16),
            pltpu.VMEM((n_k // 4, 4 * rows, 4 * rows), F32),
            pltpu.VMEM((total, share // 2, 2 * rows), F32),
            pltpu.VMEM((total, share // 2, 2 * rows), F32),
            dma((n_g,)), dma((n_k,)), dma((n_k,)), dma((n_k,)), dma((n_k,)),
            dma((n_g,)), dma((n_g,)), dma(()), dma(()),
        ]
        + [pltpu.VMEM((n_k, 2 * n_c, width), BF16)] * n_g,
        compiler_params=pltpu.CompilerParams(
            collective_id=0, has_side_effects=True, vmem_limit_bytes=48 * 1024 * 1024
        ),
        cost_estimate=pl.CostEstimate(
            flops=2 * n_k * rows * width * screen.shape[2],
            bytes_accessed=2 * width * screen.shape[2],
            transcendentals=0,
        ),
    )(cond, vale, screen, qtable, gmap)
    return result.reshape(1, NSHIFT + 1, share * rows)


def solution(mesh):
    in_specs = (P("ka", None, "ga"), P("ka", None, "ga"), P("ka", "ga", None), P(), P("ka", "ga"))
    out_specs = P("ka", None, "ga")
    return jax.shard_map(
        per_device, mesh=mesh, in_specs=in_specs, out_specs=out_specs, check_vma=False
    )
```

time: 871 us -> 36.4 us (0.04)
  waiting for transfers between devices: 749 us -> 0 us
  blocking collectives: 35.7 us -> 0 us
  Pallas kernels: 0 us -> 32.5 us
  local copies, waits for them, and re-layouts: 31.7 us -> 3.49 us
  matrix products: 18.1 us -> 0 us
  between operations: 15.5 us -> 0.01 us
  other arithmetic: 13.1 us -> 0 us
    psum x1 -> x0, waiting for transfers between devices: 705 us -> none  [broadcast(): return lax.psum(kept, axis)]
    all_gather x4 -> x0, blocking collectives: 35.7 us -> none  [the longest x3 30.4 us: per_device(): lax.all_gather(entry[1], 'ga', axis=2, tiled=True)]
    pallas_call x0 -> x1, Pallas kernels: none -> 32.5 us  [per_device(): pl.pallas_call(functools.partial(kernel, n_k, n_g), out_shape=jax.ShapeDt...]
    unnamed x3 -> x0, waiting for transfers between devices: 30.6 us -> none
    dot_general x6 -> x0, matrix products: 18.1 us -> none  [the longest x3 17.2 us: per_device(): lax.dot_general(slab, stacked, (((1,), (1,)), ((), ())), preferred_elemen...]
    unnamed x16 -> x8, local copies, waits for them, and re-layouts: 20.2 us -> 2.81 us
    ppermute x4 -> x0, waiting for transfers between devices: 13.2 us -> none  [passed_along(): lax.ppermute(array, axis, [(i, (i + by) % peers) for i in range(peers)])]
    select_n x1 -> x0, other arithmetic: 11 us -> none  [broadcast(): jnp.where(lax.axis_index(axis) == source, value, 0).astype(value.dtype)]
  transfers between devices with their start and end apart: 6 -> 0, of which waited for: 4 -> 0; matrix products, arithmetic and copies ran while one was open for 1% -> 0% of each run, Pallas kernels for 0% -> 0%
where the time goes in v1:
time: 36.4 us; the launch traced here: 36 us
  Pallas kernels  32.5 us (89%)
  local copies, waits for them, and re-layouts  3.49 us (10%)
    pallas_call x1, Pallas kernels, per_device(): pl.pallas_call(functools.partial(kernel, n_k, n_g), out_shape=jax.ShapeDt...  32.5 us
    unnamed x8, local copies, waits for them, and re-layouts  2.81 us

profile of v1, /device:TPU:0, one launch (start us, length us, event | category | flops | bytes accessed | tf_op | source)
XLA Modules:
  0.0 36.0 jit_solution(13422875620409939241)
XLA Ops:
  0.0 0.0 copy-start
  0.0 0.7 %copy-done = bf16[1,8,1024]{2,1,0:T(8,128)(2,1)S(1)} copy-done((bf16[1,8,1024]{2,1,0:T(8,128)(2,1)S(1)}, bf16[1,8,1024]{2,1,0:T(8,128)(2,1)}, u32[]{:S(2)}) %copy-start) | copy-done | bytes 16408
  0.7 0.0 copy-start.1
  0.7 0.7 %copy-done.1 = bf16[1,8,1024]{2,1,0:T(8,128)(2,1)S(1)} copy-done((bf16[1,8,1024]{2,1,0:T(8,128)(2,1)S(1)}, bf16[1,8,1024]{2,1,0:T(8,128)(2,1)}, u32[]{:S(2)}) %copy-start.1) | copy-done | bytes 16408
  1.4 0.0 copy-start.2
  1.4 0.7 %copy-done.2 = s32[8,8]{1,0:T(8,128)S(1)} copy-done((s32[8,8]{1,0:T(8,128)S(1)}, s32[8,8]{1,0:T(8,128)}, u32[]{:S(2)}) %copy-start.2) | copy-done | bytes 280
  2.1 0.0 copy-start.3
  2.1 0.7 %copy-done.3 = s32[1,1024]{1,0:T(1,128)S(1)} copy-done((s32[1,1024]{1,0:T(1,128)S(1)}, s32[1,1024]{1,0:T(1,128)}, u32[]{:S(2)}) %copy-start.3) | copy-done | bytes 4120
  2.8 32.5 %shard_map.55 = f32[3,16,64]{2,1,0:T(8,128)S(1)} custom-call(bf16[1,8,1024]{2,1,0:T(8,128)(2,1)S(1)} %copy-done, bf16[1,8,1024]{2,1,0:T(8,128)(2,1)S(1)} %copy-done.1, bf16[1,1024,4096]{2,1,0:T(8,128)(2,1)} %screen.1, s32[8,8]{1,0:T(8,128)S(1)} %copy-done.2, s32[1,1024]{1,0:T(1,128)S(1)} %copy-done.3), custom_call_target="tpu_custom_call" | custom-call | flops 4294967296 | bytes 8388608 | tf_op jit(solution)/shard_map/pallas_call | solution.py:263
  35.3 0.7 %reshape.4 = f32[1,3,1024]{2,0,1:T(1,128)} reshape(f32[3,16,64]{2,1,0:T(8,128)S(1)} %shard_map.55) | data formatting | bytes 24576 | tf_op jit(solution)/shard_map/reshape | solution.py:291
Async XLA Ops:
  0.0 0.7 %copy-start = (bf16[1,8,1024]{2,1,0:T(8,128)(2,1)S(1)}, bf16[1,8,1024]{2,1,0:T(8,128)(2,1)}, u32[]{:S(2)}) copy-start(bf16[1,8,1024]{2,1,0:T(8,128)(2,1)} %cond.1) | copy-start | bytes 49156
  0.7 0.7 %copy-start.1 = (bf16[1,8,1024]{2,1,0:T(8,128)(2,1)S(1)}, bf16[1,8,1024]{2,1,0:T(8,128)(2,1)}, u32[]{:S(2)}) copy-start(bf16[1,8,1024]{2,1,0:T(8,128)(2,1)} %vale.1) | copy-start | bytes 49156
  1.4 0.7 %copy-start.2 = (s32[8,8]{1,0:T(8,128)S(1)}, s32[8,8]{1,0:T(8,128)}, u32[]{:S(2)}) copy-start(s32[8,8]{1,0:T(8,128)} %qtable.1) | copy-start | bytes 772
  2.1 0.7 %copy-start.3 = (s32[1,1024]{1,0:T(1,128)S(1)}, s32[1,1024]{1,0:T(1,128)}, u32[]{:S(2)}) copy-start(s32[1,1024]{1,0:T(1,128)} %gmap.1) | copy-start | bytes 12292
